TPU v7x, 32 devices: a whole 2x2x4 slice. The times are simulated.
32 devices in a mesh: dp: 4 (over y, x), seq: 8 (over z, core).
Axes of the slice: x: 2, y: 2, z: 4, core: 2. Of those that a mesh axis runs over, the one named last changes fastest.
Arguments:
- hidden_u: bfloat16 [4096, 1024], P(('dp', 'seq')), may hold values from -6 to 6
- enc_rows: bfloat16 [12288, 1536], P(('dp', 'seq')), may hold values from -6 to 6
- enc_gain: float32 [1536], replicated, may hold values from 0.5 to 1.5
- enc_shift: float32 [1536], replicated, may hold values from -3 to 3
- proj_weight: bfloat16 [1024, 1024], P(('dp', 'seq')), may hold values from -0.1875 to 0.1875
- proj_bias: float32 [1024], replicated, may hold values from -3 to 3
- counts: int32 [4, 32], P('dp'), may hold values from 4 to 64, as said below
- offsets: int32 [4, 32], P('dp'), may hold values from 0 to 1023, as said below
- owners: int32 [4, 32], P('dp'), may hold values from 0 to 7, as said below
- dropped: int32 [4, 32], P('dp'), may hold values 0 or 1
- segments: int32 [4096], P(('dp', 'seq')), may hold values from 0 to 31, as said below
Outputs:
- grad_hidden: bfloat16 [4096, 1024], P(('dp', 'seq'))
- grad_weight: float32 [1024, 1024], P(('dp', 'seq'))
- grad_bias: float32 [1024], replicated
Inputs may be any that keep to these rules, and one draw needn't show every extreme that they name: A group's counts sum to 1024. `offsets`: the images' runs of tokens lie end to end in some packing order, each token in exactly one run. `owners`: the index of seq holding the image's first token or the next one; that owner's rows of enc_rows hold its images one after another in image order from its first row, rows after them are padding. `segments`: the image whose run holds the token, consistent with offsets and counts.
All inputs are finite; a program needn't handle non-finite values. No bound on the sum of `dropped` on one device may be relied on, other than what follows from the above.
Results may differ from a plain program's by a relative error of at most 0.0058.
Values may be sent and summed in bfloat16 or wider, within the bound.
A program may use at most 64 MiB of HBM per device.

v0:
```python
import jax
import jax.numpy as jnp
from jax import lax
from jax.sharding import PartitionSpec as P

NORM_EPS = 1e-06
LENGTH_EPS = 1e-06
LOSS_SCALE = 1024.0
DROP_WEIGHT = 0.5


def passed_along(value, axis, steps):
    count = lax.axis_size(axis)
    first, last = (max(0, -steps), min(count, count - steps))
    return lax.ppermute(value, axis, [(source, source + steps) for source in range(first, last)])


def layer_norm(values, enc_gain, enc_shift):
    widened = values.astype(jnp.float32)
    center = widened - jnp.mean(widened, axis=-1, keepdims=True)
    spread = jnp.mean(center * center, axis=-1, keepdims=True)
    return (center * lax.rsqrt(spread + NORM_EPS) * enc_gain + enc_shift).astype(jnp.bfloat16)


def align_grad(projected, target, weight_tok):
    widened = target.astype(jnp.float32)
    inv_proj = lax.rsqrt(jnp.sum(projected * projected, axis=1, keepdims=True) + LENGTH_EPS)
    inv_target = lax.rsqrt(jnp.sum(widened * widened, axis=1, keepdims=True) + LENGTH_EPS)
    cosine = jnp.sum(projected * widened, axis=1, keepdims=True) * inv_proj * inv_target
    factor = -LOSS_SCALE * weight_tok[:, None]
    return (
        factor * (widened * inv_proj * inv_target - cosine * projected * inv_proj * inv_proj)
    ).astype(jnp.bfloat16)


def body(
    hidden_u,
    enc_rows,
    enc_gain,
    enc_shift,
    proj_weight,
    proj_bias,
    counts,
    offsets,
    owners,
    dropped,
    segments,
):
    tok_rows = hidden_u.shape[0]
    spill_len = tok_rows // 2
    out_width = proj_weight.shape[1]
    seq_index = lax.axis_index("seq")
    image_count = counts[0]
    image_start = offsets[0]
    image_owner = owners[0]
    image_drop = dropped[0]
    images = image_count.shape[0]
    index = jnp.arange(images, dtype=jnp.int32)
    earlier = (image_owner[:, None] == image_owner[None, :]) & (index[None, :] < index[:, None])
    base_row = jnp.sum(jnp.where(earlier, image_count[None, :], 0), axis=1)
    source = layer_norm(enc_rows, enc_gain, enc_shift)[:, :out_width]

    def select(target_shard, row_total):
        places = target_shard * tok_rows + jnp.arange(row_total, dtype=jnp.int32)
        inside = (places[:, None] >= image_start[None, :]) & (
            places[:, None] < (image_start + image_count)[None, :]
        )
        from_here = inside & (image_owner == seq_index)[None, :]
        row_index = jnp.sum(
            jnp.where(from_here, (base_row - image_start)[None, :] + places[:, None], 0), axis=1
        )
        present = jnp.any(from_here, axis=1)
        picked = jnp.take(source, jnp.clip(row_index, 0, source.shape[0] - 1), axis=0)
        return jnp.where(present[:, None], picked, jnp.zeros_like(picked))

    from_next = passed_along(select(seq_index - 1, tok_rows), "seq", -1)
    from_previous = passed_along(select(seq_index + 1, spill_len), "seq", 1)
    padded_spill = jnp.concatenate(
        [
            from_previous,
            jnp.zeros((tok_rows - spill_len, from_previous.shape[1]), from_previous.dtype),
        ],
        axis=0,
    )
    target = from_next + select(seq_index, tok_rows) + padded_spill
    same_image = segments[:, None] == index[None, :]
    count_tok = jnp.sum(jnp.where(same_image, image_count[None, :], 0), axis=1).astype(jnp.float32)
    drop_tok = jnp.sum(jnp.where(same_image, image_drop[None, :], 0), axis=1)
    weight_tok = jnp.where(drop_tok == 1, DROP_WEIGHT, 1.0) / count_tok
    group_weight = lax.all_gather(proj_weight, "seq", axis=0, tiled=True)
    columns = hidden_u
    projected = (
        jnp.dot(
            columns,
            lax.all_gather(group_weight, "dp", axis=0, tiled=True),
            preferred_element_type=jnp.float32,
        )
        + proj_bias
    )
    grad_proj = align_grad(projected, target, weight_tok)
    grad_hidden = lax.dot_general(
        grad_proj,
        lax.all_gather(group_weight, "dp", axis=0, tiled=True),
        (((1,), (1,)), ((), ())),
        preferred_element_type=jnp.float32,
    ).astype(jnp.bfloat16)
    columns = hidden_u
    group_grad = lax.psum_scatter(
        lax.dot_general(
            columns, grad_proj, (((0,), (0,)), ((), ())), preferred_element_type=jnp.float32
        ),
        "dp",
        scatter_dimension=0,
        tiled=True,
    )
    grad_weight = lax.psum_scatter(group_grad, "seq", scatter_dimension=0, tiled=True)
    grad_bias = lax.psum(jnp.sum(grad_proj, axis=0, dtype=jnp.float32), ("dp", "seq"))
    return (grad_hidden, grad_weight, grad_bias)


def solution(mesh):
    placed = (
        P(("dp", "seq"), None),
        P(("dp", "seq"), None),
        P(),
        P(),
        P(("dp", "seq"), None),
        P(),
        P("dp", None),
        P("dp", None),
        P("dp", None),
        P("dp", None),
        P(("dp", "seq")),
    )
    return jax.shard_map(
        body,
        mesh=mesh,
        in_specs=placed,
        out_specs=(P(("dp", "seq"), None), P(("dp", "seq"), None), P()),
        check_vma=False,
    )
```

profile of v0, /device:TPU:0, one launch (start us, length us, event | category | flops | bytes accessed | tf_op | source)
XLA Modules:
  0.0 170.0 jit_solution(12101719561408298907)
XLA Ops:
  7.2 0.0 all-gather.2.cloned.1.call-start
  7.2 17.9 %all_gather.7 = bf16[256,1024]{1,0:T(8,128)(2,1)} all-gather(bf16[32,1024]{1,0:T(8,128)(2,1)} %param.17), channel_id=1, replica_groups=mesh['dp'=4,'seq'=8] {'seq'}, dimensions={0}, use_global_device_ids=true | all-gather | bytes 589824 | tf_op jit(solution)/shard_map/all_gather | solution.py:90
  25.2 0.0 all-gather.2.cloned.1.call-update
  25.2 0.0 reduce-scatter.5.cloned.1.call-start
  25.3 0.7 compare_bitcast_fusion
  25.9 0.9 select_reduce_fusion.3
  26.8 0.7 add_bitcast_fusion
  27.5 0.8 select_reduce_fusion
  28.3 1.5 convert_reduce_fusion
  29.8 0.4 multiply_reduce_fusion
  30.3 0.3 fusion.2
  30.6 0.7 gather_fusion
  31.3 0.1 fusion.14
  31.4 0.1 select_select_fusion.2
  31.5 2.3 %collective-permute-start.1 = (bf16[64,1024]{1,0:T(8,128)(2,1)S(1)}, bf16[64,1024]{1,0:T(8,128)(2,1)S(1)}, u32[]{:S(2)}, u32[]{:S(2)}) collective-permute-start(bf16[64,1024]{1,0:T(8,128)(2,1)S(1)} %select_select_fusion.2), channel_id=1, source_target_pairs={{0,1},{1,2},{2,3},{3,4},{4,5},{5,6},{6,7},{8,9},{9,10},{10,11},{11... | collective-permute-start | bytes 393224 | tf_op jit(solution)/shard_map/ppermute | solution.py:15
  33.8 0.1 select_reduce_fusion.1
  34.0 0.9 gather_fusion.1
  34.8 0.1 fusion.13
  34.9 0.1 select_select_fusion.1
  35.1 1.3 collective-permute-start
  36.4 0.1 select_reduce_fusion.5
  36.5 0.9 gather_fusion.2
  37.4 1.8 %collective-permute-done = bf16[128,1024]{1,0:T(8,128)(2,1)S(1)} collective-permute-done((bf16[128,1024]{1,0:T(8,128)(2,1)S(1)}, bf16[128,1024]{1,0:T(8,128)(2,1)S(1)}, u32[]{:S(2)}, u32[]{:S(2)}) %collective-permute-start) | collective-permute-done | bytes 262176 | tf_op jit(solution)/shard_map/ppermute | solution.py:15
  39.1 22.5 %all-gather.2.cloned.1.call-done = bf16[1024,1024]{1,0:T(8,128)(2,1)} async-done(((bf16[256,1024]{1,0:T(8,128)(2,1)}), bf16[1024,1024]{1,0:T(8,128)(2,1)}) %all-gather.2.cloned.1.call-update) | async-done | bytes 2097168 | tf_op jit(solution)/shard_map/all_gather | solution.py:95
  61.6 2.3 %multiply_reduce_fusion.1 = (f32[128]{0:T(128)S(1)}, f32[128]{0:T(128)S(1)}, f32[128]{0:T(128)S(1)}, bf16[128,1024]{1,0:T(8,128)(2,1)S(1)}, f32[128,1024]{1,0:T(8,128)S(1)}) fusion(bf16[64,1024]{1,0:T(8,128)(2,1)S(1)} %collective-permute-done.1, bf16[128,1024]{1,0:T(8,128)(2,1)S(1)} %collective-permute-done, bf16[128,1024]{1,0:T(8,128)(2,1)S(1)} %gather_fusion.2, ...), kind=kOutput, calls=%fused_computation.23 | convolution fusion | flops 270532224 | bytes 3806976 | tf_op jit(solution)/shard_map/dot_general | solution.py:93
  63.9 0.2 convert_reduce_fusion.1
  64.2 2.7 %convolution_bitcast_fusion = f32[1024,1024]{0,1:T(8,128)} fusion(bf16[128,1024]{1,0:T(8,128)(2,1)S(1)} %get-tuple-element.23, bf16[128,1024]{1,0:T(8,128)(2,1)S(1)} %copy-done), kind=kOutput, calls=%fused_computation.6 | convolution fusion | flops 268435456 | bytes 4718592 | tf_op jit(solution)/shard_map/dot_general | solution.py:109
  66.8 0.0 reduce-scatter.7.cloned.1.call-start
  66.9 52.7 %reduce-scatter.5.cloned.1.call-done = f32[256,1024]{0,1:T(8,128)} async-done(((f32[1024,1024]{0,1:T(8,128)}), f32[256,1024]{0,1:T(8,128)}) %reduce-scatter.5.cloned.1.call-update) | async-done | bytes 1048592 | tf_op jit(solution)/shard_map/reduce_scatter | solution.py:108
  119.6 2.5 %copy.17 = f32[256,1024]{1,0:T(8,128)} copy(f32[256,1024]{0,1:T(8,128)} %reduce-scatter.5.cloned.1.call-done) | data formatting | bytes 2097152
  122.2 39.7 %psum.7 = f32[1024]{0:T(1024)} all-reduce(f32[1024]{0:T(1024)S(1)} %get-tuple-element.22), channel_id=1, replica_groups=mesh['dp'=4,'seq'=8] {'dp','seq'}, use_global_device_ids=true, to_apply=%region_17.19 | all-reduce | flops 1024 | bytes 8192 | tf_op jit(solution)/shard_map/psum | solution.py:117
  161.9 1.5 convolution_convert_fusion
  (38 shorter events, 0.2 us)
Async XLA Ops:
  7.2 54.4 %copy-start = (bf16[128,1024]{1,0:T(8,128)(2,1)S(1)}, bf16[128,1024]{1,0:T(8,128)(2,1)}, u32[]{:S(2)}) copy-start(bf16[128,1024]{1,0:T(8,128)(2,1)} %param.13) | copy-start | bytes 786436
  7.2 22.6 %copy-start.1 = (bf16[384,1536]{1,0:T(8,128)(2,1)S(1)}, bf16[384,1536]{1,0:T(8,128)(2,1)}, u32[]{:S(2)}) copy-start(bf16[384,1536]{1,0:T(8,128)(2,1)} %param.14) | copy-start | bytes 3538948
  7.2 54.4 %all-gather.2.cloned.1.call-start = ((), (), s32[]{:S(2)}) async-start(), calls=%async_computation.2 | async-start | bytes 2621440 | tf_op jit(solution)/shard_map/all_gather | solution.py:95
  25.2 94.5 %reduce-scatter.5.cloned.1.call-start = ((), (), s32[]{:S(2)}) async-start(), calls=%async_computation.3 | async-start | bytes 5242880 | tf_op jit(solution)/shard_map/reduce_scatter | solution.py:108
  28.3 2.0 %slice-start = ((f32[1536]{0:T(1024)}), f32[1024]{0:T(1024)S(1)}, s32[]{:S(2)}) async-start(f32[1536]{0:T(1024)} %param.15), calls=%async_computation.5 | async-start | bytes 8192 | tf_op jit(solution)/shard_map/slice | solution.py:61
  28.3 2.0 %slice-start.1 = ((f32[1536]{0:T(1024)}), f32[1024]{0:T(1024)S(1)}, s32[]{:S(2)}) async-start(f32[1536]{0:T(1024)} %param.16), calls=%async_computation.6 | async-start | bytes 8192 | tf_op jit(solution)/shard_map/slice | solution.py:61
  30.3 1.0 copy-start.3
  30.6 5.8 %copy-start.4 = (s32[1,32]{1,0:T(1,128)S(1)}, s32[1,32]{1,0:T(1,128)}, u32[]{:S(2)}) copy-start(s32[1,32]{1,0:T(1,128)} %param.19) | copy-start | bytes 388
  30.6 5.8 %copy-start.5 = (s32[1,32]{1,0:T(1,128)S(1)}, s32[1,32]{1,0:T(1,128)}, u32[]{:S(2)}) copy-start(s32[1,32]{1,0:T(1,128)} %param.22) | copy-start | bytes 388
  30.6 5.8 %copy-start.6 = (s32[128]{0:T(128)S(1)}, s32[128]{0:T(128)}, u32[]{:S(2)}) copy-start(s32[128]{0:T(128)} %param.23) | copy-start | bytes 1540
  31.5 5.8 %collective-permute-start.1 = (bf16[64,1024]{1,0:T(8,128)(2,1)S(1)}, bf16[64,1024]{1,0:T(8,128)(2,1)S(1)}, u32[]{:S(2)}, u32[]{:S(2)}) collective-permute-start(bf16[64,1024]{1,0:T(8,128)(2,1)S(1)} %select_select_fusion.2), channel_id=1, source_target_pairs={{0,1},{1,2},{2,3},{3,4},{4,5},{5,6},{6,7},{8,9},{9,10},{10,11},{11... | collective-permute-start | bytes 393224 | tf_op jit(solution)/shard_map/ppermute | solution.py:15
  34.0 27.6 %copy-start.7 = (f32[1024]{0:T(1024)S(1)}, f32[1024]{0:T(1024)}, u32[]{:S(2)}) copy-start(f32[1024]{0:T(1024)} %param.18) | copy-start | bytes 12292
  35.1 4.1 %collective-permute-start = (bf16[128,1024]{1,0:T(8,128)(2,1)S(1)}, bf16[128,1024]{1,0:T(8,128)(2,1)S(1)}, u32[]{:S(2)}, u32[]{:S(2)}) collective-permute-start(bf16[128,1024]{1,0:T(8,128)(2,1)S(1)} %select_select_fusion.1), channel_id=1, source_target_pairs={{1,0},{2,1},{3,2},{4,3},{5,4},{6,5},{7,6},{9,8},{10,9},{11,10},{12... | collective-permute-start | bytes 786440 | tf_op jit(solution)/shard_map/ppermute | solution.py:15
  66.8 95.0 %copy-start.2 = (bf16[1024,1024]{1,0:T(8,128)(2,1)S(1)}, bf16[1024,1024]{1,0:T(8,128)(2,1)}, u32[]{:S(2)}) copy-start(bf16[1024,1024]{1,0:T(8,128)(2,1)} %all-gather.2.cloned.1.call-done) | copy-start | bytes 6291460
  66.8 96.6 %reduce-scatter.7.cloned.1.call-start = ((), (), s32[]{:S(2)}) async-start(), calls=%async_computation.4 | async-start | bytes 1179648
Sparse Core Ops, SparseCore 0:
  25.3 36.2 all-gather.1
  67.0 52.6 reduce-scatter.4
  122.6 32.4 reduce-scatter.6
where the time goes:
time: 170 us
  waiting for transfers between devices  77 us (45%)
  blocking collectives  57.6 us (34%)
  between operations  14 us (8%)
  matrix products  6.47 us (4%)
  other arithmetic  6.15 us (4%)
  local copies, waits for them, and re-layouts  5.04 us (3%)
  starting transfers between devices  3.67 us (2%)
    reduce_scatter x1, waiting for transfers between devices, body(): lax.psum_scatter(lax.dot_general(columns, grad_proj, (((0,), (0,)), ((),...  52.7 us
    psum x1, blocking collectives, body(): lax.psum(jnp.sum(grad_proj, axis=0, dtype=jnp.float32), ('dp', 'seq'))  39.7 us
    all_gather x1, waiting for transfers between devices, body(): lax.all_gather(group_weight, 'dp', axis=0, tiled=True)  22.5 us
    all_gather x1, blocking collectives, body(): group_weight = lax.all_gather(proj_weight, 'seq', axis=0, tiled=True)  17.9 us
    ppermute x2, starting transfers between devices, passed_along(): lax.ppermute(value, axis, [(source, source + steps) for source in range(f...  3.55 us
  transfers between devices with their start and end apart: 5, of which 3 were waited for; matrix products, arithmetic and copies ran while one was open for 6% of the time, Pallas kernels for 0%

commit v1 on v0

--- a/solution.py
+++ b/solution.py
@@ -1,6 +1,10 @@
+import functools
+
 import jax
 import jax.numpy as jnp
 from jax import lax
+from jax.experimental import pallas as pl
+from jax.experimental.pallas import tpu as pltpu
 from jax.sharding import PartitionSpec as P
 
 NORM_EPS = 1e-06
@@ -118,6 +122,396 @@
     return (grad_hidden, grad_weight, grad_bias)
 
 
+def fused_kernel(
+    n_dp,
+    n_seq,
+    hidden_ref,
+    enc_ref,
+    gain_ref,
+    shift_ref,
+    weight_ref,
+    bias_ref,
+    counts_ref,
+    offsets_ref,
+    owners_ref,
+    dropped_ref,
+    grad_hidden_ref,
+    grad_weight_ref,
+    grad_bias_ref,
+    layer,
+    source,
+    hidden_t,
+    to_prev,
+    to_next,
+    from_next,
+    from_prev,
+    target,
+    grad_proj,
+    partial,
+    pair_out,
+    pair_in,
+    dp_out,
+    dp_in,
+    own_sum,
+    z_out,
+    z_in,
+    bias_own,
+    bias_pair,
+    bias_mid,
+    bias_dp,
+    bias_last,
+    bias_z,
+    send_sem,
+    recv_sem,
+):
+    f32, bf16 = jnp.float32, jnp.bfloat16
+    n_z = n_seq // 2
+    tok_rows, depth = hidden_ref.shape
+    rows, out_width = weight_ref.shape
+    enc_cap = enc_ref.shape[0]
+    spill_len = to_next.shape[0]
+    images = counts_ref.shape[1]
+    dp = lax.axis_index("dp")
+    seq = lax.axis_index("seq")
+    z, core = seq // 2, seq % 2
+    mate_seq = z * 2 + 1 - core
+    mate = (dp, mate_seq)
+    used = []
+
+    def copy(src, dst, device):
+        slot = len(used)
+        used.append(slot)
+        return pltpu.make_async_remote_copy(
+            src_ref=src,
+            dst_ref=dst,
+            send_sem=send_sem.at[slot],
+            recv_sem=recv_sem.at[slot],
+            device_id=device,
+            device_id_type=pl.DeviceIdType.MESH,
+        )
+
+    def dp_at(k):
+        return lax.rem(dp + (k + n_dp), n_dp)
+
+    def z_at(k):
+        return lax.rem(z + (k + n_z), n_z)
+
+    def layer_rows(dp_index, z_index, core_index):
+        start = ((dp_index * n_z + z_index) * 2 + core_index) * rows
+        return layer.at[pl.ds(pl.multiple_of(start, rows), rows)]
+
+    barrier = pltpu.get_barrier_semaphore()
+    for k in range(1, n_seq):
+        pl.semaphore_signal(
+            barrier,
+            inc=1,
+            device_id=(dp, lax.rem(seq + k, n_seq)),
+            device_id_type=pl.DeviceIdType.MESH,
+        )
+    for k in range(1, n_dp):
+        pl.semaphore_signal(
+            barrier, inc=1, device_id=(dp_at(k), seq), device_id_type=pl.DeviceIdType.MESH
+        )
+    own_rows = layer_rows(dp, z, core)
+    own_rows[...] = weight_ref[...]
+    pl.semaphore_wait(barrier, n_seq + n_dp - 2)
+
+    in_flight = []
+
+    def start(src, dst, device):
+        one = copy(src, dst, device)
+        one.start()
+        in_flight.append(one)
+        return one
+
+    z_copies = {}
+    dp_copies = {}
+    mate_copies = []
+
+    def spread(kz):
+        block = layer_rows(dp, z_at(-kz), core)
+        for k in range(1, n_dp):
+            dp_copies[kz, k] = start(block, block, (dp_at(k), seq))
+        mate_copies.append(start(block, block, mate))
+
+    for kz in range(1, n_z):
+        z_copies[kz] = start(own_rows, own_rows, (dp, z_at(kz) * 2 + core))
+    spread(0)
+
+    gain = gain_ref[:, :]
+    shift = shift_ref[:, :]
+    step = 32 if enc_cap % 32 == 0 else enc_cap
+
+    def norm_step(i, carry):
+        at = pl.ds(pl.multiple_of(i * step, step), step)
+        source[at] = layer_norm(enc_ref[at], gain, shift)[:, :out_width]
+        return carry
+
+    lax.fori_loop(0, enc_cap // step, norm_step, 0)
+
+    count = counts_ref[...].astype(f32)
+    first = offsets_ref[...].astype(f32)
+    owner = owners_ref[...].astype(f32)
+    drop = dropped_ref[...].astype(f32)
+    down = lax.broadcasted_iota(jnp.int32, (images, images), 0)
+    across = lax.broadcasted_iota(jnp.int32, (images, images), 1)
+
+    def as_column(row):
+        return jnp.sum(jnp.where(down == across, row, 0.0), axis=1, keepdims=True)
+
+    earlier = (as_column(owner) == owner) & (down < across)
+    base = jnp.sum(jnp.where(earlier, as_column(count), 0.0), axis=0, keepdims=True)
+
+    def inside_of(shard, row_total):
+        places = (
+            shard * tok_rows + lax.broadcasted_iota(jnp.int32, (row_total, 1), 0)
+        ).astype(f32)
+        return places, (places >= first) & (places < first + count)
+
+    def select(shard, row_total):
+        places, inside = inside_of(shard, row_total)
+        from_here = inside & (owner == seq.astype(f32))
+        row_index = jnp.sum(
+            jnp.where(from_here, base - first + places + 1.0, 0.0), axis=1, keepdims=True
+        )
+        lanes = lax.broadcasted_iota(jnp.int32, (row_total, enc_cap), 1).astype(f32)
+        chosen = jnp.where(lanes + 1.0 == row_index, 1.0, 0.0).astype(bf16)
+        return jnp.dot(chosen, source[...], preferred_element_type=f32)
+
+    to_prev[...] = select(seq - 1, tok_rows).astype(bf16)
+    prev_copy = copy(to_prev, from_next, (dp, jnp.maximum(seq - 1, 0)))
+
+    @pl.when(seq > 0)
+    def _():
+        prev_copy.start()
+
+    to_next[...] = select(seq + 1, spill_len).astype(bf16)
+    next_copy = copy(to_next, from_prev, (dp, jnp.minimum(seq + 1, n_seq - 1)))
+
+    @pl.when(seq < n_seq - 1)
+    def _():
+        next_copy.start()
+
+    for kz in range(1, n_z):
+        z_copies[kz].wait_recv()
+        spread(kz)
+
+    target[...] = select(seq, tok_rows)
+    hidden_t[...] = hidden_ref[...].T
+
+    for kz in range(n_z):
+        for k in range(1, n_dp):
+            dp_copies[kz, k].wait_recv()
+            block = layer_rows(dp_at(-k), z_at(-kz), core)
+            mate_copies.append(start(block, block, mate))
+
+    @pl.when(seq < n_seq - 1)
+    def _():
+        prev_copy.wait_recv()
+        target[...] += from_next[...].astype(f32)
+
+    @pl.when(seq > 0)
+    def _():
+        next_copy.wait_recv()
+        target[:spill_len] += from_prev[...].astype(f32)
+
+    for one in mate_copies:
+        one.wait_recv()
+
+    _, inside = inside_of(seq, tok_rows)
+    count_tok = jnp.sum(jnp.where(inside, count, 0.0), axis=1, keepdims=True)
+    drop_tok = jnp.sum(jnp.where(inside, drop, 0.0), axis=1, keepdims=True)
+    weight_tok = jnp.where(drop_tok == 1.0, DROP_WEIGHT, 1.0) / count_tok
+    projected = jnp.dot(hidden_ref[...], layer[...], preferred_element_type=f32) + bias_ref[...]
+    widened = target[...]
+    inv_proj = lax.rsqrt(jnp.sum(projected * projected, axis=1, keepdims=True) + LENGTH_EPS)
+    inv_target = lax.rsqrt(jnp.sum(widened * widened, axis=1, keepdims=True) + LENGTH_EPS)
+    cosine = jnp.sum(projected * widened, axis=1, keepdims=True) * inv_proj * inv_target
+    factor = -LOSS_SCALE * weight_tok
+    grad_proj[...] = (
+        factor * (widened * inv_proj * inv_target - cosine * projected * inv_proj * inv_proj)
+    ).astype(bf16)
+
+    bias_own[...] = jnp.sum(grad_proj[...].astype(f32), axis=0, keepdims=True)
+    bias_mate = start(bias_own, bias_pair, mate)
+
+    chunk = depth // n_dp
+
+    def partial_step(i, carry):
+        at = pl.ds(pl.multiple_of(i * chunk, chunk), chunk)
+        partial[at] = jnp.dot(hidden_t[at], grad_proj[...], preferred_element_type=f32)
+        return carry
+
+    lax.fori_loop(0, n_dp, partial_step, 0)
+
+    def partial_rows(dp_index, z_index, core_index):
+        begin = ((dp_index * n_z + z_index) * 2 + core_index) * rows
+        return partial[pl.ds(pl.multiple_of(begin, rows), rows)]
+
+    order = list(range(1, n_z)) + [0]
+    pair_copies = {}
+    for kz in order:
+        for k in range(n_dp):
+            pair_out[kz, k] = partial_rows(dp_at(k), z_at(kz), 1 - core).astype(bf16)
+        pair_copies[kz] = start(pair_out.at[kz], pair_in.at[kz], mate)
+
+    bias_mate.wait_recv()
+    bias_mid[...] = bias_own[...] + bias_pair[...]
+    bias_dp[pl.ds(dp, 1)] = bias_mid[...][None]
+    bias_dp_copies = [
+        start(bias_mid, bias_dp.at[dp], (dp_at(k), seq)) for k in range(1, n_dp)
+    ]
+
+    sum_copies = {}
+    for kz in order:
+        pair_copies[kz].wait_recv()
+        for k in range(1, n_dp):
+            total = partial_rows(dp_at(k), z_at(kz), core) + pair_in[kz, k].astype(f32)
+            dp_out[kz, k - 1] = total.astype(bf16)
+            sum_copies[kz, k] = start(
+                dp_out.at[kz, k - 1], dp_in.at[kz, k - 1], (dp_at(k), seq)
+            )
+        own_sum[kz] = partial_rows(dp, z_at(kz), core) + pair_in[kz, 0].astype(f32)
+
+    for one in bias_dp_copies:
+        one.wait_recv()
+    summed = bias_dp[0]
+    for k in range(1, n_dp):
+        summed += bias_dp[k]
+    bias_last[...] = summed
+    bias_z[pl.ds(z, 1)] = summed[None]
+    bias_z_copies = [
+        start(bias_last, bias_z.at[z], (dp, z_at(kz) * 2 + core)) for kz in range(1, n_z)
+    ]
+
+    grad_hidden_ref[...] = lax.dot_general(
+        grad_proj[...], layer[...], (((1,), (1,)), ((), ())), preferred_element_type=f32
+    ).astype(bf16)
+
+    last_copies = []
+    for kz in order:
+        total = own_sum[kz]
+        for k in range(1, n_dp):
+            sum_copies[kz, k].wait_recv()
+            total += dp_in[kz, k - 1].astype(f32)
+        if kz:
+            z_out[kz - 1] = total.astype(bf16)
+            last_copies.append(
+                start(z_out.at[kz - 1], z_in.at[kz - 1], (dp, z_at(kz) * 2 + core))
+            )
+        else:
+            own_sum[0] = total
+
+    for one in bias_z_copies:
+        one.wait_recv()
+    summed = bias_z[0]
+    for kz in range(1, n_z):
+        summed += bias_z[kz]
+    grad_bias_ref[...] = summed
+
+    total = own_sum[0]
+    for at, one in enumerate(last_copies):
+        one.wait_recv()
+        total += z_in[at].astype(f32)
+    grad_weight_ref[...] = total
+
+    for one in in_flight:
+        one.wait_send()
+
+    @pl.when(seq > 0)
+    def _():
+        prev_copy.wait_send()
+
+    @pl.when(seq < n_seq - 1)
+    def _():
+        next_copy.wait_send()
+
+
+def fused_body(
+    hidden_u,
+    enc_rows,
+    enc_gain,
+    enc_shift,
+    proj_weight,
+    proj_bias,
+    counts,
+    offsets,
+    owners,
+    dropped,
+    segments,
+):
+    n_dp, n_seq = lax.axis_size("dp"), lax.axis_size("seq")
+    n_z = n_seq // 2
+    tok_rows, depth = hidden_u.shape
+    rows, out_width = proj_weight.shape
+    enc_cap = enc_rows.shape[0]
+    spill_len = tok_rows // 2
+    f32, bf16 = jnp.float32, jnp.bfloat16
+    copies = 3 * n_z * n_dp + 2 * n_z + n_z * n_dp + 4 * n_z + 2 * n_dp + 8
+    vmem = pl.BlockSpec(memory_space=pltpu.VMEM)
+    grad_hidden, grad_weight, grad_bias = pl.pallas_call(
+        functools.partial(fused_kernel, n_dp, n_seq),
+        out_shape=(
+            jax.ShapeDtypeStruct((tok_rows, depth), bf16),
+            jax.ShapeDtypeStruct((rows, out_width), f32),
+            jax.ShapeDtypeStruct((1, out_width), f32),
+        ),
+        in_specs=[vmem] * 10,
+        out_specs=(vmem, vmem, vmem),
+        scratch_shapes=[
+            pltpu.VMEM((depth, out_width), bf16),
+            pltpu.VMEM((enc_cap, out_width), bf16),
+            pltpu.VMEM((depth, tok_rows), bf16),
+            pltpu.VMEM((tok_rows, out_width), bf16),
+            pltpu.VMEM((spill_len, out_width), bf16),
+            pltpu.VMEM((tok_rows, out_width), bf16),
+            pltpu.VMEM((spill_len, out_width), bf16),
+            pltpu.VMEM((tok_rows, out_width), f32),
+            pltpu.VMEM((tok_rows, out_width), bf16),
+            pltpu.VMEM((depth, out_width), f32),
+            pltpu.VMEM((n_z, n_dp, rows, out_width), bf16),
+            pltpu.VMEM((n_z, n_dp, rows, out_width), bf16),
+            pltpu.VMEM((n_z, n_dp - 1, rows, out_width), bf16),
+            pltpu.VMEM((n_z, n_dp - 1, rows, out_width), bf16),
+            pltpu.VMEM((n_z, rows, out_width), f32),
+            pltpu.VMEM((n_z - 1, rows, out_width), bf16),
+            pltpu.VMEM((n_z - 1, rows, out_width), bf16),
+            pltpu.VMEM((1, out_width), f32),
+            pltpu.VMEM((1, out_width), f32),
+            pltpu.VMEM((1, out_width), f32),
+            pltpu.VMEM((n_dp, 1, out_width), f32),
+            pltpu.VMEM((1, out_width), f32),
+            pltpu.VMEM((n_z, 1, out_width), f32),
+            pltpu.SemaphoreType.DMA((copies,)),
+            pltpu.SemaphoreType.DMA((copies,)),
+        ],
+        compiler_params=pltpu.CompilerParams(
+            collective_id=0, has_side_effects=True, vmem_limit_bytes=48 * 1024 * 1024
+        ),
+    )(
+        hidden_u,
+        enc_rows,
+        enc_gain[None, :],
+        enc_shift[None, :],
+        proj_weight,
+        proj_bias[None, :],
+        counts,
+        offsets,
+        owners,
+        dropped,
+    )
+    return grad_hidden, grad_weight, grad_bias[0]
+
+
+def either(*arrays):
+    rows, tokens = arrays[4].shape[0], arrays[0].shape[0]
+    n_dp, n_seq = lax.axis_size("dp"), lax.axis_size("seq")
+    whole_tiles = rows % 16 == 0 and tokens % 32 == 0
+    if whole_tiles and n_seq % 2 == 0 and n_seq >= 4 and n_dp >= 2:
+        return fused_body(*arrays)
+    return body(*arrays)
+
+
 def solution(mesh):
     placed = (
         P(("dp", "seq"), None),
@@ -133,7 +527,7 @@
         P(("dp", "seq")),
     )
     return jax.shard_map(
-        body,
+        either,
         mesh=mesh,
         in_specs=placed,
         out_specs=(P(("dp", "seq"), None), P(("dp", "seq"), None), P()),

time: 170 us -> 50.7 us (0.30)
  waiting for transfers between devices: 77 us -> 0 us
  blocking collectives: 57.6 us -> 0 us
  Pallas kernels: 0 us -> 40 us
  between operations: 14 us -> 0.65 us
  matrix products: 6.47 us -> 0 us
  other arithmetic: 6.15 us -> 0 us
  local copies, waits for them, and re-layouts: 5.04 us -> 9.72 us
  starting transfers between devices: 3.67 us -> 0 us
    reduce_scatter x1 -> x0, waiting for transfers between devices: 52.7 us -> none  [body(): lax.psum_scatter(lax.dot_general(columns, grad_proj, (((0,), (0,)), ((),...]
    pallas_call x0 -> x1, Pallas kernels: none -> 40 us  [fused_body(): pl.pallas_call(functools.partial(fused_kernel, n_dp, n_seq), out_shape=(j...]
    psum x1 -> x0, blocking collectives: 39.7 us -> none  [body(): lax.psum(jnp.sum(grad_proj, axis=0, dtype=jnp.float32), ('dp', 'seq'))]
    all_gather x1 -> x0, waiting for transfers between devices: 22.5 us -> none  [body(): lax.all_gather(group_weight, 'dp', axis=0, tiled=True)]
    all_gather x1 -> x0, blocking collectives: 17.9 us -> none  [body(): group_weight = lax.all_gather(proj_weight, 'seq', axis=0, tiled=True)]
    dot_general x3 -> x0, matrix products: 6.47 us -> none  [the longest x1 2.66 us: body(): lax.dot_general(columns, grad_proj, (((0,), (0,)), ((), ())), preferred_e...]
    unnamed x17 -> x19, local copies, waits for them, and re-layouts: 2.6 us -> 8.32 us
    reduce_sum x7 -> x0, other arithmetic: 4.05 us -> none  [the longest x1 1.51 us: layer_norm(): center = widened - jnp.mean(widened, axis=-1, keepdims=True)]
  transfers between devices with their start and end apart: 5 -> 0, of which waited for: 3 -> 0; matrix products, arithmetic and copies ran while one was open for 6% -> 0% of each run, Pallas kernels for 0% -> 0%
where the time goes in v1:
time: 50.7 us; the launch traced here: 50.3 us
  Pallas kernels  40 us (79%)
  local copies, waits for them, and re-layouts  9.72 us (19%)
  between operations  0.65 us (1%)
    pallas_call x1, Pallas kernels, fused_body(): pl.pallas_call(functools.partial(fused_kernel, n_dp, n_seq), out_shape=(j...  40 us
    unnamed x19, local copies, waits for them, and re-layouts  8.32 us

profile of v1, /device:TPU:0, one launch (start us, length us, event | category | flops | bytes accessed | tf_op | source)
XLA Modules:
  0.0 50.3 jit_solution(4007161471115437604)
XLA Ops:
  0.6 0.7 %broadcast_in_dim.9.gain_ref = f32[1,1536]{1,0:T(1,128)S(1)} reshape(f32[1536]{0:T(1024)} %param.13) | data formatting | bytes 12288 | tf_op jit(solution)/shard_map/broadcast_in_dim | solution.py:494
  1.3 0.7 %broadcast_in_dim.10.shift_ref = f32[1,1536]{1,0:T(1,128)S(1)} reshape(f32[1536]{0:T(1024)} %param.14) | data formatting | bytes 12288 | tf_op jit(solution)/shard_map/broadcast_in_dim | solution.py:495
  2.0 0.0 copy-start
  2.0 1.3 %copy-done = bf16[384,1536]{1,0:T(8,128)(2,1)S(1)} copy-done((bf16[384,1536]{1,0:T(8,128)(2,1)S(1)}, bf16[384,1536]{1,0:T(8,128)(2,1)}, u32[]{:S(2)}) %copy-start) | copy-done | bytes 1179672
  3.3 0.0 copy-start.1
  3.3 0.9 %copy-done.1 = bf16[128,1024]{1,0:T(8,128)(2,1)S(1)} copy-done((bf16[128,1024]{1,0:T(8,128)(2,1)S(1)}, bf16[128,1024]{1,0:T(8,128)(2,1)}, u32[]{:S(2)}) %copy-start.1) | copy-done | bytes 262168
  4.3 0.0 copy-start.2
  4.3 0.8 %copy-done.2 = bf16[32,1024]{1,0:T(8,128)(2,1)S(1)} copy-done((bf16[32,1024]{1,0:T(8,128)(2,1)S(1)}, bf16[32,1024]{1,0:T(8,128)(2,1)}, u32[]{:S(2)}) %copy-start.2) | copy-done | bytes 65560
  5.1 0.0 copy-start.3
  5.1 0.7 %copy-done.3 = f32[1024]{0:T(1024)S(1)} copy-done((f32[1024]{0:T(1024)S(1)}, f32[1024]{0:T(1024)}, u32[]{:S(2)}) %copy-start.3) | copy-done | bytes 4120
  5.8 0.0 copy-start.4
  5.8 0.7 %copy-done.4 = s32[1,32]{1,0:T(1,128)S(1)} copy-done((s32[1,32]{1,0:T(1,128)S(1)}, s32[1,32]{1,0:T(1,128)}, u32[]{:S(2)}) %copy-start.4) | copy-done | bytes 152
  6.4 0.0 copy-start.5
  6.4 0.7 %copy-done.5 = s32[1,32]{1,0:T(1,128)S(1)} copy-done((s32[1,32]{1,0:T(1,128)S(1)}, s32[1,32]{1,0:T(1,128)}, u32[]{:S(2)}) %copy-start.5) | copy-done | bytes 152
  7.1 0.0 copy-start.6
  7.1 0.7 %copy-done.6 = s32[1,32]{1,0:T(1,128)S(1)} copy-done((s32[1,32]{1,0:T(1,128)S(1)}, s32[1,32]{1,0:T(1,128)}, u32[]{:S(2)}) %copy-start.6) | copy-done | bytes 152
  7.8 0.0 copy-start.7
  7.8 0.7 %copy-done.7 = s32[1,32]{1,0:T(1,128)S(1)} copy-done((s32[1,32]{1,0:T(1,128)S(1)}, s32[1,32]{1,0:T(1,128)}, u32[]{:S(2)}) %copy-start.7) | copy-done | bytes 152
  8.4 40.0 %shard_map.121 = (bf16[128,1024]{1,0:T(8,128)(2,1)S(1)}, f32[32,1024]{1,0:T(8,128)S(1)}, f32[1,1024]{1,0:T(1,128)S(1)}) custom-call(bf16[128,1024]{1,0:T(8,128)(2,1)S(1)} %copy-done.1, bf16[384,1536]{1,0:T(8,128)(2,1)S(1)} %copy-done, f32[1,1536]{1,0:T(1,128)S(1)} %broadcast_in_dim.9.gain_ref, f32[1,1536]{1,0:T(1,128)S(1)} %broadcast_in_dim.10.shift_ref, ...), custom_call_target="tpu_custom_call" | custom-call | tf_op jit(solution)/shard_map/pallas_call | solution.py:452
  48.4 0.7 %copy.16 = bf16[128,1024]{1,0:T(8,128)(2,1)} copy(bf16[128,1024]{1,0:T(8,128)(2,1)S(1)} %get-tuple-element.12) | data formatting | bytes 524288
  49.1 0.7 %copy.17 = f32[32,1024]{1,0:T(8,128)} copy(f32[32,1024]{1,0:T(8,128)S(1)} %get-tuple-element.13) | data formatting | bytes 262144
  49.8 0.6 %copy.18 = f32[1024]{0:T(1024)} copy(f32[1024]{0:T(1024)S(1)} %bitcast.3) | data formatting | bytes 8192
Async XLA Ops:
  2.0 1.3 %copy-start = (bf16[384,1536]{1,0:T(8,128)(2,1)S(1)}, bf16[384,1536]{1,0:T(8,128)(2,1)}, u32[]{:S(2)}) copy-start(bf16[384,1536]{1,0:T(8,128)(2,1)} %enc_ref.1) | copy-start | bytes 3538948
  3.3 0.9 %copy-start.1 = (bf16[128,1024]{1,0:T(8,128)(2,1)S(1)}, bf16[128,1024]{1,0:T(8,128)(2,1)}, u32[]{:S(2)}) copy-start(bf16[128,1024]{1,0:T(8,128)(2,1)} %hidden_ref.1) | copy-start | bytes 786436
  4.3 0.8 %copy-start.2 = (bf16[32,1024]{1,0:T(8,128)(2,1)S(1)}, bf16[32,1024]{1,0:T(8,128)(2,1)}, u32[]{:S(2)}) copy-start(bf16[32,1024]{1,0:T(8,128)(2,1)} %weight_ref.1) | copy-start | bytes 196612
  5.1 0.7 %copy-start.3 = (f32[1024]{0:T(1024)S(1)}, f32[1024]{0:T(1024)}, u32[]{:S(2)}) copy-start(f32[1024]{0:T(1024)} %param.16) | copy-start | bytes 12292
  5.8 0.7 %copy-start.4 = (s32[1,32]{1,0:T(1,128)S(1)}, s32[1,32]{1,0:T(1,128)}, u32[]{:S(2)}) copy-start(s32[1,32]{1,0:T(1,128)} %counts_ref.1) | copy-start | bytes 388
  6.4 0.7 %copy-start.5 = (s32[1,32]{1,0:T(1,128)S(1)}, s32[1,32]{1,0:T(1,128)}, u32[]{:S(2)}) copy-start(s32[1,32]{1,0:T(1,128)} %offsets_ref.1) | copy-start | bytes 388
  7.1 0.7 %copy-start.6 = (s32[1,32]{1,0:T(1,128)S(1)}, s32[1,32]{1,0:T(1,128)}, u32[]{:S(2)}) copy-start(s32[1,32]{1,0:T(1,128)} %owners_ref.1) | copy-start | bytes 388
  7.8 0.7 %copy-start.7 = (s32[1,32]{1,0:T(1,128)S(1)}, s32[1,32]{1,0:T(1,128)}, u32[]{:S(2)}) copy-start(s32[1,32]{1,0:T(1,128)} %dropped_ref.1) | copy-start | bytes 388

commit v2 on v1

--- a/solution.py
+++ b/solution.py
@@ -125,16 +125,16 @@
 def fused_kernel(
     n_dp,
     n_seq,
-    hidden_ref,
-    enc_ref,
-    gain_ref,
-    shift_ref,
-    weight_ref,
-    bias_ref,
-    counts_ref,
-    offsets_ref,
-    owners_ref,
-    dropped_ref,
+    hidden_hbm,
+    enc_hbm,
+    gain_hbm,
+    shift_hbm,
+    weight_hbm,
+    bias_hbm,
+    counts_hbm,
+    offsets_hbm,
+    owners_hbm,
+    dropped_hbm,
     grad_hidden_ref,
     grad_weight_ref,
     grad_bias_ref,
@@ -161,13 +161,23 @@
     bias_dp,
     bias_last,
     bias_z,
+    hidden_ref,
+    enc_ref,
+    gain_ref,
+    shift_ref,
+    bias_ref,
+    counts_ref,
+    offsets_ref,
+    owners_ref,
+    dropped_ref,
     send_sem,
     recv_sem,
+    load_sem,
 ):
     f32, bf16 = jnp.float32, jnp.bfloat16
     n_z = n_seq // 2
     tok_rows, depth = hidden_ref.shape
-    rows, out_width = weight_ref.shape
+    rows, out_width = weight_hbm.shape
     enc_cap = enc_ref.shape[0]
     spill_len = to_next.shape[0]
     images = counts_ref.shape[1]
@@ -190,7 +200,14 @@
             device_id_type=pl.DeviceIdType.MESH,
         )
 
+    square = n_dp == 4
+
     def dp_at(k):
+        if square:
+            k = abs(k)
+            across_x = 1 - 2 * lax.rem(dp, 2)
+            across_y = 2 - 4 * (dp // 2)
+            return dp + (across_x if k % 2 else 0) + (across_y if k // 2 else 0)
         return lax.rem(dp + (k + n_dp), n_dp)
 
     def z_at(k):
@@ -213,7 +230,22 @@
             barrier, inc=1, device_id=(dp_at(k), seq), device_id_type=pl.DeviceIdType.MESH
         )
     own_rows = layer_rows(dp, z, core)
-    own_rows[...] = weight_ref[...]
+    loads = []
+    for src, dst in (
+        (weight_hbm, own_rows),
+        (enc_hbm, enc_ref),
+        (gain_hbm, gain_ref),
+        (shift_hbm, shift_ref),
+        (counts_hbm, counts_ref),
+        (offsets_hbm, offsets_ref),
+        (owners_hbm, owners_ref),
+        (dropped_hbm, dropped_ref),
+        (hidden_hbm, hidden_ref),
+        (bias_hbm, bias_ref),
+    ):
+        loads.append(pltpu.make_async_copy(src, dst, load_sem.at[len(loads)]))
+        loads[-1].start()
+    loads[0].wait()
     pl.semaphore_wait(barrier, n_seq + n_dp - 2)
 
     in_flight = []
@@ -224,13 +256,14 @@
         in_flight.append(one)
         return one
 
+    direct = (1, 2) if square else range(1, n_dp)
     z_copies = {}
     dp_copies = {}
     mate_copies = []
 
     def spread(kz):
         block = layer_rows(dp, z_at(-kz), core)
-        for k in range(1, n_dp):
+        for k in direct:
             dp_copies[kz, k] = start(block, block, (dp_at(k), seq))
         mate_copies.append(start(block, block, mate))
 
@@ -238,8 +271,10 @@
         z_copies[kz] = start(own_rows, own_rows, (dp, z_at(kz) * 2 + core))
     spread(0)
 
-    gain = gain_ref[:, :]
-    shift = shift_ref[:, :]
+    for one in loads[1:]:
+        one.wait()
+    gain = gain_ref[...][None, :]
+    shift = shift_ref[...][None, :]
     step = 32 if enc_cap % 32 == 0 else enc_cap
 
     def norm_step(i, carry):
@@ -300,9 +335,16 @@
     hidden_t[...] = hidden_ref[...].T
 
     for kz in range(n_z):
-        for k in range(1, n_dp):
+        for k in direct:
             dp_copies[kz, k].wait_recv()
             block = layer_rows(dp_at(-k), z_at(-kz), core)
+            if square and k == 1 + kz % 2:
+                dp_copies[kz, 3] = start(block, block, (dp_at(3 - k), seq))
+            mate_copies.append(start(block, block, mate))
+    if square:
+        for kz in range(n_z):
+            dp_copies[kz, 3].wait_recv()
+            block = layer_rows(dp_at(3), z_at(-kz), core)
             mate_copies.append(start(block, block, mate))
 
     @pl.when(seq < n_seq - 1)
@@ -322,7 +364,7 @@
     count_tok = jnp.sum(jnp.where(inside, count, 0.0), axis=1, keepdims=True)
     drop_tok = jnp.sum(jnp.where(inside, drop, 0.0), axis=1, keepdims=True)
     weight_tok = jnp.where(drop_tok == 1.0, DROP_WEIGHT, 1.0) / count_tok
-    projected = jnp.dot(hidden_ref[...], layer[...], preferred_element_type=f32) + bias_ref[...]
+    projected = jnp.dot(hidden_ref[...], layer[...], preferred_element_type=f32) + bias_ref[...][None, :]
     widened = target[...]
     inv_proj = lax.rsqrt(jnp.sum(projected * projected, axis=1, keepdims=True) + LENGTH_EPS)
     inv_target = lax.rsqrt(jnp.sum(widened * widened, axis=1, keepdims=True) + LENGTH_EPS)
@@ -456,7 +498,7 @@
             jax.ShapeDtypeStruct((rows, out_width), f32),
             jax.ShapeDtypeStruct((1, out_width), f32),
         ),
-        in_specs=[vmem] * 10,
+        in_specs=[pl.BlockSpec(memory_space=pltpu.HBM)] * 10,
         out_specs=(vmem, vmem, vmem),
         scratch_shapes=[
             pltpu.VMEM((depth, out_width), bf16),
@@ -482,19 +524,29 @@
             pltpu.VMEM((n_dp, 1, out_width), f32),
             pltpu.VMEM((1, out_width), f32),
             pltpu.VMEM((n_z, 1, out_width), f32),
+            pltpu.VMEM(hidden_u.shape, bf16),
+            pltpu.VMEM(enc_rows.shape, bf16),
+            pltpu.VMEM(enc_gain.shape, f32),
+            pltpu.VMEM(enc_shift.shape, f32),
+            pltpu.VMEM(proj_bias.shape, f32),
+            pltpu.VMEM(counts.shape, jnp.int32),
+            pltpu.VMEM(offsets.shape, jnp.int32),
+            pltpu.VMEM(owners.shape, jnp.int32),
+            pltpu.VMEM(dropped.shape, jnp.int32),
             pltpu.SemaphoreType.DMA((copies,)),
             pltpu.SemaphoreType.DMA((copies,)),
+            pltpu.SemaphoreType.DMA((10,)),
         ],
         compiler_params=pltpu.CompilerParams(
-            collective_id=0, has_side_effects=True, vmem_limit_bytes=48 * 1024 * 1024
+            collective_id=0, has_side_effects=True, vmem_limit_bytes=60 * 1024 * 1024
         ),
     )(
         hidden_u,
         enc_rows,
-        enc_gain[None, :],
-        enc_shift[None, :],
+        enc_gain,
+        enc_shift,
         proj_weight,
-        proj_bias[None, :],
+        proj_bias,
         counts,
         offsets,
         owners,

time: 50.7 us -> 47.2 us (0.931)
  local copies, waits for them, and re-layouts: 9.72 us -> 4.5 us
  Pallas kernels: 40 us -> 41.8 us
    unnamed x19 -> x3, local copies, waits for them, and re-layouts: 8.32 us -> 4.5 us
    pallas_call x1, Pallas kernels: 40 us -> 41.8 us  [fused_body(): pl.pallas_call(functools.partial(fused_kernel, n_dp, n_seq), out_shape=(j...]
    broadcast_in_dim x2 -> x0, local copies, waits for them, and re-layouts: 1.4 us -> none  [the longest x1 0.7 us: fused_body(): enc_gain[None, :]]
where the time goes in v2:
time: 47.2 us; the launch traced here: 47 us
  Pallas kernels  41.8 us (89%)
  local copies, waits for them, and re-layouts  4.5 us (10%)
  between operations  0.64 us (1%)
    pallas_call x1, Pallas kernels, fused_body(): pl.pallas_call(functools.partial(fused_kernel, n_dp, n_seq), out_shape=(j...  41.8 us
    unnamed x3, local copies, waits for them, and re-layouts  4.5 us

profile of v2, /device:TPU:0, one launch (start us, length us, event | category | flops | bytes accessed | tf_op | source)
XLA Modules:
  0.0 47.0 jit_solution(6431172981986045431)
XLA Ops:
  0.6 41.8 %shard_map.121 = (bf16[128,1024]{1,0:T(8,128)(2,1)}, f32[32,1024]{1,0:T(8,128)}, f32[1,1024]{1,0:T(1,128)}) custom-call(bf16[128,1024]{1,0:T(8,128)(2,1)} %hidden_hbm.1, bf16[384,1536]{1,0:T(8,128)(2,1)} %enc_hbm.1, f32[1536]{0:T(1024)} %gain_hbm.1, f32[1536]{0:T(1024)} %shift_hbm.1, bf16[32,1024]{1,0:T(8,128)(2,1)} %weight_hbm.1, f32[1024]{0:T(1024)} %bias_hbm.1, ...), custom_call_target="tpu_custom_call" | custom-call | tf_op jit(solution)/shard_map/pallas_call | solution.py:494
  42.5 1.7 %copy.16 = bf16[128,1024]{1,0:T(8,128)(2,1)} copy(bf16[128,1024]{1,0:T(8,128)(2,1)} %get-tuple-element.12) | data formatting | bytes 524288
  44.1 1.6 %copy.17 = f32[32,1024]{1,0:T(8,128)} copy(f32[32,1024]{1,0:T(8,128)} %get-tuple-element.13) | data formatting | bytes 262144
  45.7 1.3 %copy.18 = f32[1024]{0:T(1024)} copy(f32[1024]{0:T(1024)} %bitcast.1) | data formatting | bytes 8192

commit v3 on v2

--- a/solution.py
+++ b/solution.py
@@ -494,9 +494,9 @@
     grad_hidden, grad_weight, grad_bias = pl.pallas_call(
         functools.partial(fused_kernel, n_dp, n_seq),
         out_shape=(
-            jax.ShapeDtypeStruct((tok_rows, depth), bf16),
-            jax.ShapeDtypeStruct((rows, out_width), f32),
-            jax.ShapeDtypeStruct((1, out_width), f32),
+            pltpu.VMEM((tok_rows, depth), bf16),
+            pltpu.VMEM((rows, out_width), f32),
+            pltpu.VMEM((1, out_width), f32),
         ),
         in_specs=[pl.BlockSpec(memory_space=pltpu.HBM)] * 10,
         out_specs=(vmem, vmem, vmem),
@@ -538,7 +538,7 @@
             pltpu.SemaphoreType.DMA((10,)),
         ],
         compiler_params=pltpu.CompilerParams(
-            collective_id=0, has_side_effects=True, vmem_limit_bytes=60 * 1024 * 1024
+            collective_id=0, has_side_effects=True, vmem_limit_bytes=54 * 1024 * 1024
         ),
     )(
         hidden_u,

time: 47.2 us -> 43.8 us (0.928)
  local copies, waits for them, and re-layouts: 4.5 us -> 1.95 us
  Pallas kernels: 41.8 us -> 41.1 us
    unnamed x3, local copies, waits for them, and re-layouts: 4.5 us -> 1.95 us
    pallas_call x1, Pallas kernels: 41.8 us -> 41.1 us  [fused_body(): pl.pallas_call(functools.partial(fused_kernel, n_dp, n_seq), out_shape=(p...]
where the time goes in v3:
time: 43.8 us; the launch traced here: 43.7 us
  Pallas kernels  41.1 us (94%)
  local copies, waits for them, and re-layouts  1.95 us (4%)
  between operations  0.64 us (1%)
    pallas_call x1, Pallas kernels, fused_body(): pl.pallas_call(functools.partial(fused_kernel, n_dp, n_seq), out_shape=(p...  41.1 us
    unnamed x3, local copies, waits for them, and re-layouts  1.95 us

profile of v3, /device:TPU:0, one launch (start us, length us, event | category | flops | bytes accessed | tf_op | source)
XLA Modules:
  0.0 43.7 jit_solution(9541403429480133114)
XLA Ops:
  0.6 41.1 %shard_map.121 = (bf16[128,1024]{1,0:T(8,128)(2,1)S(1)}, f32[32,1024]{1,0:T(8,128)S(1)}, f32[1,1024]{1,0:T(1,128)S(1)}) custom-call(bf16[128,1024]{1,0:T(8,128)(2,1)} %hidden_hbm.1, bf16[384,1536]{1,0:T(8,128)(2,1)} %enc_hbm.1, f32[1536]{0:T(1024)} %gain_hbm.1, f32[1536]{0:T(1024)} %shift_hbm.1, bf16[32,1024]{1,0:T(8,128)(2,1)} %weight_hbm.1, ...), custom_call_target="tpu_custom_call" | custom-call | tf_op jit(solution)/shard_map/pallas_call | solution.py:494
  41.7 0.7 %copy.16 = bf16[128,1024]{1,0:T(8,128)(2,1)} copy(bf16[128,1024]{1,0:T(8,128)(2,1)S(1)} %get-tuple-element.9) | data formatting | bytes 524288
  42.4 0.6 %copy.18 = f32[1024]{0:T(1024)} copy(f32[1024]{0:T(1024)S(1)} %bitcast.1) | data formatting | bytes 8192
  43.0 0.7 %copy.17 = f32[32,1024]{1,0:T(8,128)} copy(f32[32,1024]{1,0:T(8,128)S(1)} %get-tuple-element.10) | data formatting | bytes 262144

commit v4 on v3

--- a/solution.py
+++ b/solution.py
@@ -170,6 +170,8 @@
     offsets_ref,
     owners_ref,
     dropped_ref,
+    hidden_z,
+    side_sum,
     send_sem,
     recv_sem,
     load_sem,
@@ -282,7 +284,12 @@
         source[at] = layer_norm(enc_ref[at], gain, shift)[:, :out_width]
         return carry
 
-    lax.fori_loop(0, enc_cap // step, norm_step, 0)
+    norm_steps = enc_cap // step
+    lax.fori_loop(0, norm_steps // 3, norm_step, 0)
+    for kz in range(1, n_z):
+        z_copies[kz].wait_recv()
+        spread(kz)
+    lax.fori_loop(norm_steps // 3, norm_steps, norm_step, 0)
 
     count = counts_ref[...].astype(f32)
     first = offsets_ref[...].astype(f32)
@@ -326,13 +333,6 @@
     @pl.when(seq < n_seq - 1)
     def _():
         next_copy.start()
-
-    for kz in range(1, n_z):
-        z_copies[kz].wait_recv()
-        spread(kz)
-
-    target[...] = select(seq, tok_rows)
-    hidden_t[...] = hidden_ref[...].T
 
     for kz in range(n_z):
         for k in direct:
@@ -346,6 +346,15 @@
             dp_copies[kz, 3].wait_recv()
             block = layer_rows(dp_at(3), z_at(-kz), core)
             mate_copies.append(start(block, block, mate))
+
+    target[...] = select(seq, tok_rows)
+    hidden_t[...] = hidden_ref[...].T
+    for kz in range(n_z):
+        for k in range(n_dp):
+            begin = (dp_at(k) * n_z + z_at(kz)) * 2 * rows
+            hidden_z[kz, k * 2 * rows : (k + 1) * 2 * rows] = hidden_t[
+                pl.ds(pl.multiple_of(begin, rows), 2 * rows)
+            ]
 
     @pl.when(seq < n_seq - 1)
     def _():
@@ -377,24 +386,16 @@
     bias_own[...] = jnp.sum(grad_proj[...].astype(f32), axis=0, keepdims=True)
     bias_mate = start(bias_own, bias_pair, mate)
 
-    chunk = depth // n_dp
-
-    def partial_step(i, carry):
-        at = pl.ds(pl.multiple_of(i * chunk, chunk), chunk)
-        partial[at] = jnp.dot(hidden_t[at], grad_proj[...], preferred_element_type=f32)
-        return carry
-
-    lax.fori_loop(0, n_dp, partial_step, 0)
-
-    def partial_rows(dp_index, z_index, core_index):
-        begin = ((dp_index * n_z + z_index) * 2 + core_index) * rows
-        return partial[pl.ds(pl.multiple_of(begin, rows), rows)]
+    def partial_rows(kz, k, core_index):
+        begin = (k * 2 + core_index) * rows
+        return partial[kz, pl.ds(pl.multiple_of(begin, rows), rows)]
 
     order = list(range(1, n_z)) + [0]
     pair_copies = {}
     for kz in order:
+        partial[kz] = jnp.dot(hidden_z[kz], grad_proj[...], preferred_element_type=f32)
         for k in range(n_dp):
-            pair_out[kz, k] = partial_rows(dp_at(k), z_at(kz), 1 - core).astype(bf16)
+            pair_out[kz, k] = partial_rows(kz, k, 1 - core).astype(bf16)
         pair_copies[kz] = start(pair_out.at[kz], pair_in.at[kz], mate)
 
     bias_mate.wait_recv()
@@ -404,16 +405,35 @@
         start(bias_mid, bias_dp.at[dp], (dp_at(k), seq)) for k in range(1, n_dp)
     ]
 
+    def pair_total(kz, k):
+        return partial_rows(kz, k, core) + pair_in[kz, k].astype(f32)
+
     sum_copies = {}
     for kz in order:
         pair_copies[kz].wait_recv()
-        for k in range(1, n_dp):
-            total = partial_rows(dp_at(k), z_at(kz), core) + pair_in[kz, k].astype(f32)
-            dp_out[kz, k - 1] = total.astype(bf16)
-            sum_copies[kz, k] = start(
-                dp_out.at[kz, k - 1], dp_in.at[kz, k - 1], (dp_at(k), seq)
+        if square:
+            one, two = 1 + kz % 2, 2 - kz % 2
+            dp_out[kz, 0] = pair_total(kz, one).astype(bf16)
+            dp_out[kz, 1] = pair_total(kz, 3).astype(bf16)
+            sum_copies[kz, 1] = start(
+                dp_out.at[kz, pl.ds(0, 2)], dp_in.at[kz, pl.ds(0, 2)], (dp_at(one), seq)
             )
-        own_sum[kz] = partial_rows(dp, z_at(kz), core) + pair_in[kz, 0].astype(f32)
+            side_sum[kz] = pair_total(kz, two)
+        else:
+            for k in range(1, n_dp):
+                dp_out[kz, k - 1] = pair_total(kz, k).astype(bf16)
+                sum_copies[kz, k] = start(
+                    dp_out.at[kz, k - 1], dp_in.at[kz, k - 1], (dp_at(k), seq)
+                )
+        own_sum[kz] = pair_total(kz, 0)
+    if square:
+        for kz in order:
+            sum_copies[kz, 1].wait_recv()
+            dp_out[kz, 2] = (side_sum[kz] + dp_in[kz, 1].astype(f32)).astype(bf16)
+            sum_copies[kz, 2] = start(
+                dp_out.at[kz, 2], dp_in.at[kz, 2], (dp_at(2 - kz % 2), seq)
+            )
+            own_sum[kz] += dp_in[kz, 0].astype(f32)
 
     for one in bias_dp_copies:
         one.wait_recv()
@@ -433,9 +453,13 @@
     last_copies = []
     for kz in order:
         total = own_sum[kz]
-        for k in range(1, n_dp):
-            sum_copies[kz, k].wait_recv()
-            total += dp_in[kz, k - 1].astype(f32)
+        if square:
+            sum_copies[kz, 2].wait_recv()
+            total += dp_in[kz, 2].astype(f32)
+        else:
+            for k in range(1, n_dp):
+                sum_copies[kz, k].wait_recv()
+                total += dp_in[kz, k - 1].astype(f32)
         if kz:
             z_out[kz - 1] = total.astype(bf16)
             last_copies.append(
@@ -510,7 +534,7 @@
             pltpu.VMEM((spill_len, out_width), bf16),
             pltpu.VMEM((tok_rows, out_width), f32),
             pltpu.VMEM((tok_rows, out_width), bf16),
-            pltpu.VMEM((depth, out_width), f32),
+            pltpu.VMEM((n_z, n_dp * 2 * rows, out_width), f32),
             pltpu.VMEM((n_z, n_dp, rows, out_width), bf16),
             pltpu.VMEM((n_z, n_dp, rows, out_width), bf16),
             pltpu.VMEM((n_z, n_dp - 1, rows, out_width), bf16),
@@ -533,6 +557,8 @@
             pltpu.VMEM(offsets.shape, jnp.int32),
             pltpu.VMEM(owners.shape, jnp.int32),
             pltpu.VMEM(dropped.shape, jnp.int32),
+            pltpu.VMEM((n_z, n_dp * 2 * rows, tok_rows), bf16),
+            pltpu.VMEM((n_z, rows, out_width), f32),
             pltpu.SemaphoreType.DMA((copies,)),
             pltpu.SemaphoreType.DMA((copies,)),
             pltpu.SemaphoreType.DMA((10,)),

time: 43.8 us -> 44.2 us (level)
  no operation moved by 1% of the time
where the time goes in v4:
time: 44.2 us; the launch traced here: 44 us
  Pallas kernels  41.4 us (94%)
  local copies, waits for them, and re-layouts  1.95 us (4%)
  between operations  0.64 us (1%)
    pallas_call x1, Pallas kernels, fused_body(): pl.pallas_call(functools.partial(fused_kernel, n_dp, n_seq), out_shape=(p...  41.4 us
    unnamed x3, local copies, waits for them, and re-layouts  1.95 us

profile of v4, /device:TPU:0, one launch (start us, length us, event | category | flops | bytes accessed | tf_op | source)
XLA Modules:
  0.0 44.0 jit_solution(13843370132887619573)
XLA Ops:
  0.6 41.4 %shard_map.121 = (bf16[128,1024]{1,0:T(8,128)(2,1)S(1)}, f32[32,1024]{1,0:T(8,128)S(1)}, f32[1,1024]{1,0:T(1,128)S(1)}) custom-call(bf16[128,1024]{1,0:T(8,128)(2,1)} %hidden_hbm.1, bf16[384,1536]{1,0:T(8,128)(2,1)} %enc_hbm.1, f32[1536]{0:T(1024)} %gain_hbm.1, f32[1536]{0:T(1024)} %shift_hbm.1, bf16[32,1024]{1,0:T(8,128)(2,1)} %weight_hbm.1, ...), custom_call_target="tpu_custom_call" | custom-call | tf_op jit(solution)/shard_map/pallas_call | solution.py:518
  42.1 0.7 %copy.16 = bf16[128,1024]{1,0:T(8,128)(2,1)} copy(bf16[128,1024]{1,0:T(8,128)(2,1)S(1)} %get-tuple-element.9) | data formatting | bytes 524288
  42.8 0.6 %copy.18 = f32[1024]{0:T(1024)} copy(f32[1024]{0:T(1024)S(1)} %bitcast.1) | data formatting | bytes 8192
  43.4 0.7 %copy.17 = f32[32,1024]{1,0:T(8,128)} copy(f32[32,1024]{1,0:T(8,128)S(1)} %get-tuple-element.10) | data formatting | bytes 262144
